TPU v7x, 128 devices: a whole 4x4x4 slice. The times are simulated.
128 devices in a mesh: row: 8 (over y, core), col: 16 (over z, x).
Axes of the slice: x: 4, y: 4, z: 4, core: 2. Of those that a mesh axis runs over, the one named last changes fastest.
Arguments:
- sigma_top: float32 [6144, 6144], P('row', 'col')
- factor_cross: float32 [6144, 6144], P('row', 'col'), may hold values from -0.078125 to 0.078125
- factor_inverse: float32 [6144, 6144], P('row', 'col')
- block_inverse: float32 [6144, 6144], P('row', 'col')
- ancestors: int32 [12], replicated, may hold values from 0 to 23, as said below
Outputs:
- sigma_cross: float32 [6144, 6144], P('row', 'col')
- sigma_child: float32 [6144, 6144], P('row', 'col')
Inputs may be any that keep to these rules, and one draw needn't show every extreme that they name: `ancestors`: 12 distinct block numbers; block 0 and block 23 are always among them.
All inputs are finite; a program needn't handle non-finite values.
Results may differ from a plain program's by a relative error of at most 0.000078.
Values sent between devices are 32-bit elements; how exact they have to be, the bound alone decides.
No kernel may reach another device: no remote copies, remote signals or barrier semaphores. Data moves between devices by JAX's collectives and lax.ppermute only.
A program may use at most 128 MiB of HBM per device.

v0:
```python
import jax
import jax.numpy as jnp
import numpy as np
from jax import lax
from jax.sharding import Mesh, PartitionSpec as P

NB = 24
NANC = 12
ROW = ("y", "core")
COL = ("z", "x")
ALL = ("y", "core", "z", "x")


def shift(x, axis, n, k):
    return lax.ppermute(x, axis, [(i, (i + k) % n) for i in range(n)])


def gather_rows(x):
    y, core = (lax.axis_index("y"), lax.axis_index("core"))
    half = x.shape[0] // 2
    left = shift(x, "y", 4, 1)
    right = shift(x, "y", 4, -1)
    far = jnp.concatenate([shift(left[:half], "y", 4, 1), shift(right[half:], "y", 4, -1)])
    mine = [x, left, right, far]
    at = [y, (y + 3) % 4, (y + 1) % 4, (y + 2) % 4]
    out = [(2 * a + core, t) for a, t in zip(at, mine)]
    out += [(2 * a + 1 - core, shift(t, "core", 2, 1)) for a, t in zip(at, mine)]
    return out


def spread(x):
    h, w = x.shape
    sub = h // 24
    return lax.all_to_all(x.reshape(3, 8, sub, w), ROW, 1, 0, tiled=True).reshape(NB, sub, w)


def pick(x, ancestors):
    return jnp.concatenate([lax.dynamic_slice_in_dim(x, ancestors[i], 1, 0) for i in range(NANC)])


def dot(a, b, dims):
    return lax.dot_general(
        a, b, (dims, ((), ())), precision=lax.Precision.HIGH, preferred_element_type=jnp.float32
    )


def per_device(sigma_top, factor_cross, factor_inverse, block_inverse, ancestors):
    h, w = sigma_top.shape
    sub = h // 24
    part = NANC * sub
    f = pick(spread(factor_cross), ancestors).reshape(part, w)
    f_all = lax.all_gather(f, COL, axis=1, tiled=True)
    strip = jnp.zeros((8 * h, w), jnp.float32)
    for r, t in gather_rows(factor_inverse):
        strip = lax.dynamic_update_slice(strip, t, (r * h, 0))
    s = pick(spread(sigma_top), ancestors).reshape(part, w)
    s_all = lax.all_gather(s, COL, axis=1, tiled=True)
    u = dot(f_all, strip, ((1,), (0,)))
    moved = lax.ppermute(
        u, ALL, [(16 * r + c, 16 * (c // 2) + 2 * r + c % 2) for r in range(8) for c in range(16)]
    )
    u_side = lax.all_gather(moved, COL, axis=0, tiled=False).reshape(8, 2, part, w)
    u_col = jnp.zeros((NANC, 8, sub, w), jnp.float32)
    for r, t in gather_rows(u):
        u_col = lax.dynamic_update_slice(u_col, t.reshape(NANC, 1, sub, w), (0, r, 0, 0))
    s_sel = jnp.concatenate(
        [lax.dynamic_slice_in_dim(s_all, ancestors[i] * 8 * sub, 8 * sub, 1) for i in range(NANC)],
        axis=1,
    )
    sigma = -dot(s_sel, u_col.reshape(8 * part, w), ((1,), (0,)))
    sigma_col = jnp.zeros((8, part, w), jnp.float32)
    for r, t in gather_rows(sigma):
        sigma_col = lax.dynamic_update_slice(sigma_col, t[None], (r, 0, 0))
    correction = jnp.concatenate([dot(u_side[:, p], sigma_col, ((0, 1), (0, 1))) for p in range(2)])
    sigma_child = block_inverse - correction
    blocks = sigma.reshape(NANC, sub, w)
    hit = ancestors[None, :] == lax.iota(jnp.int32, NB)[:, None]
    place = jnp.argmax(hit, axis=1)
    living = jnp.any(hit, axis=1)
    full = jnp.concatenate([lax.dynamic_slice_in_dim(blocks, place[b], 1, 0) for b in range(NB)])
    full = jnp.where(living[:, None, None], full, jnp.float32(0.0))
    back = lax.all_to_all(full.reshape(8, 3, sub, w), ROW, 0, 0, tiled=True)
    sigma_cross = back.reshape(8, 3, sub, w).transpose(1, 0, 2, 3).reshape(h, w)
    return (sigma_cross, sigma_child)


def solution(mesh):
    fine = Mesh(np.asarray(mesh.devices).reshape(4, 2, 4, 4), ALL)
    tile = P(ROW, COL)
    return jax.shard_map(
        per_device,
        mesh=fine,
        in_specs=(tile, tile, tile, tile, P()),
        out_specs=(tile, tile),
        check_vma=False,
    )
```

profile of v0, /device:TPU:1, one launch (start us, length us, event | category | flops | bytes accessed | tf_op | source)
XLA Modules:
  0.0 343.1 jit_solution(14482909959101323158)
XLA Ops:
  9.6 6.0 %all-to-all-start.1 = ((f32[3,8,32,384]{3,2,0,1:T(8,128)}), f32[3,8,32,384]{3,2,0,1:T(8,128)S(1)}, u32[]{:S(2)}, u32[]{:S(2)}) async-start(f32[3,8,32,384]{3,2,0,1:T(8,128)} %copy.63), calls=%async_computation.1 | async-start | bytes 2359296 | tf_op jit(solution)/shard_map/all_to_all | solution.py:34
  16.7 15.4 %all-to-all-done.1 = f32[3,8,32,384]{3,2,0,1:T(8,128)S(1)} async-done(((f32[3,8,32,384]{3,2,0,1:T(8,128)}), f32[3,8,32,384]{3,2,0,1:T(8,128)S(1)}, u32[]{:S(2)}, u32[]{:S(2)}) %all-to-all-start.1) | async-done | bytes 1179680 | tf_op jit(solution)/shard_map/all_to_all | solution.py:34
  32.1 4.3 %all-to-all-start = ((f32[3,8,32,384]{3,2,0,1:T(8,128)}), f32[3,8,32,384]{3,2,0,1:T(8,128)S(1)}, u32[]{:S(2)}, u32[]{:S(2)}) async-start(f32[3,8,32,384]{3,2,0,1:T(8,128)} %copy.62), calls=%async_computation | async-start | bytes 2359296 | tf_op jit(solution)/shard_map/all_to_all | solution.py:34
  64.1 26.1 %collective-permute-done = f32[768,384]{1,0:T(8,128)S(1)} collective-permute-done((f32[768,384]{1,0:T(8,128)}, f32[768,384]{1,0:T(8,128)S(1)}, u32[]{:S(2)}, u32[]{:S(2)}) %collective-permute-start) | collective-permute-done | bytes 1179680 | tf_op jit(solution)/shard_map/ppermute | solution.py:15
  90.4 2.7 collective-permute-start.3
  95.2 10.4 %collective-permute-done.2 = f32[384,384]{1,0:T(8,128)S(1)} collective-permute-done((f32[384,384]{1,0:T(8,128)S(1)}, f32[384,384]{1,0:T(8,128)S(1)}, u32[]{:S(2)}, u32[]{:S(2)}) %collective-permute-start.2) | collective-permute-done | bytes 589856 | tf_op jit(solution)/shard_map/ppermute | solution.py:15
  107.5 4.3 %broadcast_in_dim.53 = f32[6144,384]{1,0:T(8,128)} broadcast(f32[]{:T(128)} %constant.74.clone.1), dimensions={} | broadcast | bytes 9437188 | tf_op jit(solution)/shard_map/broadcast_in_dim | solution.py:53
  127.2 11.1 %all-gather.7.cloned.1.call-done = f32[384,6144]{1,0:T(8,128)} async-done(((f32[384,384]{1,0:T(8,128)}), f32[384,6144]{1,0:T(8,128)}) %all-gather.7.cloned.1.call-update) | async-done | bytes 9437200 | tf_op jit(solution)/shard_map/all_gather | solution.py:52
  138.3 11.7 %fusion.8 = f32[384,384]{1,0:T(8,128)S(1)} fusion(f32[384,6144]{1,0:T(8,128)} %all-gather.7.cloned.1.call-done, f32[6144,384]{1,0:T(8,128)} %constant_dynamic-update-slice_fusion.62), kind=kOutput, calls=%fused_computation.105 | convolution fusion | flops 5435817984 | bytes 19464192 | tf_op jit(solution)/shard_map/dot_general | solution.py:42
  150.0 5.2 %collective-permute-start.16 = (f32[384,384]{1,0:T(8,128)S(1)}, f32[384,384]{1,0:T(8,128)S(1)}, u32[]{:S(2)}, u32[]{:S(2)}) collective-permute-start(f32[384,384]{1,0:T(8,128)S(1)} %fusion.8), channel_id=1, source_target_pairs={{0,0},{1,1},{2,16},{3,17},{4,32},{5,33},{6,48},{7,49},{8,64},{9,65... | collective-permute-start | bytes 1769480 | tf_op jit(solution)/shard_map/ppermute | solution.py:59
  155.2 14.5 %collective-permute-done.16 = f32[384,384]{1,0:T(8,128)S(1)} collective-permute-done((f32[384,384]{1,0:T(8,128)S(1)}, f32[384,384]{1,0:T(8,128)S(1)}, u32[]{:S(2)}, u32[]{:S(2)}) %collective-permute-start.16) | collective-permute-done | bytes 589856 | tf_op jit(solution)/shard_map/ppermute | solution.py:59
  225.2 4.2 %collective-permute-start.8 = (f32[384,384]{1,0:T(8,128)S(1)}, f32[384,384]{1,0:T(8,128)S(1)}, u32[]{:S(2)}, u32[]{:S(2)}) collective-permute-start(f32[384,384]{1,0:T(8,128)S(1)} %fusion.8), channel_id=1, source_target_pairs={{0,32},{32,64},{64,96},{96,0},{1,33},{33,65},{65,97},{97,1},{2,34}... | collective-permute-start | bytes 1769480 | tf_op jit(solution)/shard_map/ppermute | solution.py:15
  229.4 4.4 %collective-permute-start.9 = (f32[384,384]{1,0:T(8,128)S(1)}, f32[384,384]{1,0:T(8,128)S(1)}, u32[]{:S(2)}, u32[]{:S(2)}) collective-permute-start(f32[384,384]{1,0:T(8,128)S(1)} %fusion.8), channel_id=1, source_target_pairs={{0,96},{32,0},{64,32},{96,64},{1,97},{33,1},{65,33},{97,65},{2,98}... | collective-permute-start | bytes 1769480 | tf_op jit(solution)/shard_map/ppermute | solution.py:15
  233.8 9.4 %collective-permute-start.12 = (f32[384,384]{1,0:T(8,128)S(1)}, f32[384,384]{1,0:T(8,128)S(1)}, u32[]{:S(2)}, u32[]{:S(2)}) collective-permute-start(f32[384,384]{1,0:T(8,128)S(1)} %fusion.8), channel_id=1, source_target_pairs={{0,16},{16,0},{1,17},{17,1},{2,18},{18,2},{3,19},{19,3},{4,20},{20... | collective-permute-start | bytes 1769480 | tf_op jit(solution)/shard_map/ppermute | solution.py:15
  255.5 2.7 collective-permute-start.11
  260.1 4.4 %collective-permute-done.10 = f32[192,384]{1,0:T(8,128)S(1)} collective-permute-done((f32[192,384]{1,0:T(8,128)S(1)}, f32[192,384]{1,0:T(8,128)S(1)}, u32[]{:S(2)}, u32[]{:S(2)}) %collective-permute-start.10) | collective-permute-done | bytes 294944 | tf_op jit(solution)/shard_map/ppermute | solution.py:15
  269.8 5.0 %bitcast_dynamic-update-slice_fusion.7 = (f32[8,384,384]{2,1,0:T(8,128)}, f32[384,384]{1,0:T(8,128)S(1)}) fusion(f32[8,384,384]{2,1,0:T(8,128)} %broadcast_in_dim.55, s32[]{:T(128)S(6)} %select_n.283, f32[384,3072]{1,0:T(8,128)S(1)} %dynamic-slice_dynamic-update-slice_fusion, f32[3072,384]{1,0:T(8,128)S(1)} %bitcast.119), kind=kOutput, calls=%fused_computation.15 | convolution fusion | flops 2718056448 | bytes 10616836 | tf_op jit(solution)/shard_map/dot_general | solution.py:42
  275.4 2.9 collective-permute-start.18
  280.5 3.5 %all-to-all-start.2 = ((f32[8,3,32,384]{3,2,1,0:T(8,128)}), f32[8,3,32,384]{3,2,1,0:T(8,128)S(1)}, u32[]{:S(2)}, u32[]{:S(2)}) async-start(f32[8,3,32,384]{3,2,1,0:T(8,128)} %broadcast_select_fusion), calls=%async_computation.2 | async-start | bytes 2359296 | tf_op jit(solution)/shard_map/all_to_all | solution.py:82
  284.0 7.7 %collective-permute-done.17 = f32[384,384]{1,0:T(8,128)S(1)} collective-permute-done((f32[384,384]{1,0:T(8,128)S(1)}, f32[384,384]{1,0:T(8,128)S(1)}, u32[]{:S(2)}, u32[]{:S(2)}) %collective-permute-start.17) | collective-permute-done | bytes 589856 | tf_op jit(solution)/shard_map/ppermute | solution.py:15
  292.0 3.7 %collective-permute-start.20 = (f32[192,384]{1,0:T(8,128)S(1)}, f32[192,384]{1,0:T(8,128)S(1)}, u32[]{:S(2)}, u32[]{:S(2)}) collective-permute-start(f32[192,384]{1,0:T(8,128)S(1)} %slice.206), channel_id=1, source_target_pairs={{0,96},{32,0},{64,32},{96,64},{1,97},{33,1},{65,33},{97,65},{2,98}... | collective-permute-start | bytes 884744 | tf_op jit(solution)/shard_map/ppermute | solution.py:15
  299.6 11.1 %collective-permute-done.19 = f32[192,384]{1,0:T(8,128)S(1)} collective-permute-done((f32[192,384]{1,0:T(8,128)S(1)}, f32[192,384]{1,0:T(8,128)S(1)}, u32[]{:S(2)}, u32[]{:S(2)}) %collective-permute-start.19) | collective-permute-done | bytes 294944 | tf_op jit(solution)/shard_map/ppermute | solution.py:15
  321.5 7.8 %fusion.2 = f32[384,384]{1,0:T(8,128)S(1)} fusion(f32[8,384,384]{2,1,0:T(8,128)} %bitcast_dynamic-update-slice_fusion, f32[8,2,384,384]{3,2,1,0:T(8,128)} %bitcast.120), kind=kOutput, calls=%fused_computation.4 | convolution fusion | flops 2717908992 | bytes 10027008 | tf_op jit(solution)/shard_map/dot_general | solution.py:42
  329.3 6.1 %fusion.3 = f32[384,384]{1,0:T(8,128)S(1)} fusion(f32[8,384,384]{2,1,0:T(8,128)} %bitcast_dynamic-update-slice_fusion, f32[8,2,384,384]{3,2,1,0:T(8,128)S(1)} %bitcast.121), kind=kOutput, calls=%fused_computation.5 | convolution fusion | flops 2717908992 | bytes 10027008 | tf_op jit(solution)/shard_map/dot_general | solution.py:42
  (167 shorter events, 69.7 us)
Async XLA Ops:
  9.6 22.5 %all-to-all-start.1 = ((f32[3,8,32,384]{3,2,0,1:T(8,128)}), f32[3,8,32,384]{3,2,0,1:T(8,128)S(1)}, u32[]{:S(2)}, u32[]{:S(2)}) async-start(f32[3,8,32,384]{3,2,0,1:T(8,128)} %copy.63), calls=%async_computation.1 | async-start | bytes 2359296 | tf_op jit(solution)/shard_map/all_to_all | solution.py:34
  32.1 26.9 %all-to-all-start = ((f32[3,8,32,384]{3,2,0,1:T(8,128)}), f32[3,8,32,384]{3,2,0,1:T(8,128)S(1)}, u32[]{:S(2)}, u32[]{:S(2)}) async-start(f32[3,8,32,384]{3,2,0,1:T(8,128)} %copy.62), calls=%async_computation | async-start | bytes 2359296 | tf_op jit(solution)/shard_map/all_to_all | solution.py:34
  36.5 101.8 %all-gather.7.cloned.1.call-start = ((), (), s32[]{:S(2)}) async-start(), calls=%async_computation.4 | async-start | bytes 10027008 | tf_op jit(solution)/shard_map/all_gather | solution.py:52
  60.2 183.0 %all-gather.5.cloned.1.call-start = ((), (), s32[]{:S(2)}) async-start(), calls=%async_computation.3 | async-start | bytes 10027008 | tf_op jit(solution)/shard_map/all_gather | solution.py:57
  61.3 260.2 %all-gather.9.cloned.1.call-start = ((), (), s32[]{:S(2)}) async-start(), calls=%async_computation.5 | async-start | bytes 10027008 | tf_op jit(solution)/shard_map/all_gather | solution.py:62
  61.3 28.9 %collective-permute-start = (f32[768,384]{1,0:T(8,128)}, f32[768,384]{1,0:T(8,128)S(1)}, u32[]{:S(2)}, u32[]{:S(2)}) collective-permute-start(f32[768,384]{1,0:T(8,128)} %param.7), channel_id=1, source_target_pairs={{0,32},{32,64},{64,96},{96,0},{1,33},{33,65},{65,97},{97,1},{2,34}... | collective-permute-start | bytes 3538952 | tf_op jit(solution)/shard_map/ppermute | solution.py:15
  62.8 27.6 %collective-permute-start.1 = (f32[768,384]{1,0:T(8,128)}, f32[768,384]{1,0:T(8,128)S(1)}, u32[]{:S(2)}, u32[]{:S(2)}) collective-permute-start(f32[768,384]{1,0:T(8,128)} %param.7), channel_id=1, source_target_pairs={{0,96},{32,0},{64,32},{96,64},{1,97},{33,1},{65,33},{97,65},{2,98}... | collective-permute-start | bytes 3538952 | tf_op jit(solution)/shard_map/ppermute | solution.py:15
  90.3 15.3 %collective-permute-start.2 = (f32[384,384]{1,0:T(8,128)S(1)}, f32[384,384]{1,0:T(8,128)S(1)}, u32[]{:S(2)}, u32[]{:S(2)}) collective-permute-start(f32[384,384]{1,0:T(8,128)S(1)} %slice.200), channel_id=1, source_target_pairs={{0,32},{32,64},{64,96},{96,0},{1,33},{33,65},{65,97},{97,1},{2,34}... | collective-permute-start | bytes 1769480 | tf_op jit(solution)/shard_map/ppermute | solution.py:15
  93.1 24.4 %collective-permute-start.4 = (f32[768,384]{1,0:T(8,128)}, f32[768,384]{1,0:T(8,128)}, u32[]{:S(2)}, u32[]{:S(2)}) collective-permute-start(f32[768,384]{1,0:T(8,128)} %param.7), channel_id=1, source_target_pairs={{0,16},{16,0},{1,17},{17,1},{2,18},{18,2},{3,19},{19,3},{4,20},{20... | collective-permute-start | bytes 3538952 | tf_op jit(solution)/shard_map/ppermute | solution.py:15
  94.7 25.3 %collective-permute-start.5 = (f32[768,384]{1,0:T(8,128)S(1)}, f32[768,384]{1,0:T(8,128)}, u32[]{:S(2)}, u32[]{:S(2)}) collective-permute-start(f32[768,384]{1,0:T(8,128)S(1)} %collective-permute-done), channel_id=1, source_target_pairs={{0,16},{16,0},{1,17},{17,1},{2,18},{18,2},{3,19},{19,3},{4,20},{20... | collective-permute-start | bytes 3538952 | tf_op jit(solution)/shard_map/ppermute | solution.py:15
  94.7 27.7 %collective-permute-start.6 = (f32[768,384]{1,0:T(8,128)S(1)}, f32[768,384]{1,0:T(8,128)}, u32[]{:S(2)}, u32[]{:S(2)}) collective-permute-start(f32[768,384]{1,0:T(8,128)S(1)} %collective-permute-done.1), channel_id=1, source_target_pairs={{0,16},{16,0},{1,17},{17,1},{2,18},{18,2},{3,19},{19,3},{4,20},{20... | collective-permute-start | bytes 3538952 | tf_op jit(solution)/shard_map/ppermute | solution.py:15
  105.6 19.2 %collective-permute-start.7 = (f32[768,384]{1,0:T(8,128)S(1)}, f32[768,384]{1,0:T(8,128)}, u32[]{:S(2)}, u32[]{:S(2)}) collective-permute-start(f32[768,384]{1,0:T(8,128)S(1)} %constant_dynamic-update-slice_fusion.24), channel_id=1, source_target_pairs={{0,16},{16,0},{1,17},{17,1},{2,18},{18,2},{3,19},{19,3},{4,20},{20... | collective-permute-start | bytes 3538952 | tf_op jit(solution)/shard_map/ppermute | solution.py:15
  150.0 19.7 %collective-permute-start.16 = (f32[384,384]{1,0:T(8,128)S(1)}, f32[384,384]{1,0:T(8,128)S(1)}, u32[]{:S(2)}, u32[]{:S(2)}) collective-permute-start(f32[384,384]{1,0:T(8,128)S(1)} %fusion.8), channel_id=1, source_target_pairs={{0,0},{1,1},{2,16},{3,17},{4,32},{5,33},{6,48},{7,49},{8,64},{9,65... | collective-permute-start | bytes 1769480 | tf_op jit(solution)/shard_map/ppermute | solution.py:59
  225.2 29.1 %collective-permute-start.8 = (f32[384,384]{1,0:T(8,128)S(1)}, f32[384,384]{1,0:T(8,128)S(1)}, u32[]{:S(2)}, u32[]{:S(2)}) collective-permute-start(f32[384,384]{1,0:T(8,128)S(1)} %fusion.8), channel_id=1, source_target_pairs={{0,32},{32,64},{64,96},{96,0},{1,33},{33,65},{65,97},{97,1},{2,34}... | collective-permute-start | bytes 1769480 | tf_op jit(solution)/shard_map/ppermute | solution.py:15
  229.4 26.1 %collective-permute-start.9 = (f32[384,384]{1,0:T(8,128)S(1)}, f32[384,384]{1,0:T(8,128)S(1)}, u32[]{:S(2)}, u32[]{:S(2)}) collective-permute-start(f32[384,384]{1,0:T(8,128)S(1)} %fusion.8), channel_id=1, source_target_pairs={{0,96},{32,0},{64,32},{96,64},{1,97},{33,1},{65,33},{97,65},{2,98}... | collective-permute-start | bytes 1769480 | tf_op jit(solution)/shard_map/ppermute | solution.py:15
  233.8 32.0 %collective-permute-start.12 = (f32[384,384]{1,0:T(8,128)S(1)}, f32[384,384]{1,0:T(8,128)S(1)}, u32[]{:S(2)}, u32[]{:S(2)}) collective-permute-start(f32[384,384]{1,0:T(8,128)S(1)} %fusion.8), channel_id=1, source_target_pairs={{0,16},{16,0},{1,17},{17,1},{2,18},{18,2},{3,19},{19,3},{4,20},{20... | collective-permute-start | bytes 1769480 | tf_op jit(solution)/shard_map/ppermute | solution.py:15
  274.9 16.9 %collective-permute-start.17 = (f32[384,384]{1,0:T(8,128)S(1)}, f32[384,384]{1,0:T(8,128)S(1)}, u32[]{:S(2)}, u32[]{:S(2)}) collective-permute-start(f32[384,384]{1,0:T(8,128)S(1)} %get-tuple-element.41), channel_id=1, source_target_pairs={{0,32},{32,64},{64,96},{96,0},{1,33},{33,65},{65,97},{97,1},{2,34}... | collective-permute-start | bytes 1769480 | tf_op jit(solution)/shard_map/ppermute | solution.py:15
  275.4 16.7 %collective-permute-start.18 = (f32[384,384]{1,0:T(8,128)S(1)}, f32[384,384]{1,0:T(8,128)S(1)}, u32[]{:S(2)}, u32[]{:S(2)}) collective-permute-start(f32[384,384]{1,0:T(8,128)S(1)} %get-tuple-element.41), channel_id=1, source_target_pairs={{0,96},{32,0},{64,32},{96,64},{1,97},{33,1},{65,33},{97,65},{2,98}... | collective-permute-start | bytes 1769480 | tf_op jit(solution)/shard_map/ppermute | solution.py:15
  278.2 34.5 %collective-permute-start.21 = (f32[384,384]{1,0:T(8,128)S(1)}, f32[384,384]{1,0:T(8,128)}, u32[]{:S(2)}, u32[]{:S(2)}) collective-permute-start(f32[384,384]{1,0:T(8,128)S(1)} %get-tuple-element.41), channel_id=1, source_target_pairs={{0,16},{16,0},{1,17},{17,1},{2,18},{18,2},{3,19},{19,3},{4,20},{20... | collective-permute-start | bytes 1769480 | tf_op jit(solution)/shard_map/ppermute | solution.py:15
  280.5 34.1 %all-to-all-start.2 = ((f32[8,3,32,384]{3,2,1,0:T(8,128)}), f32[8,3,32,384]{3,2,1,0:T(8,128)S(1)}, u32[]{:S(2)}, u32[]{:S(2)}) async-start(f32[8,3,32,384]{3,2,1,0:T(8,128)} %broadcast_select_fusion), calls=%async_computation.2 | async-start | bytes 2359296 | tf_op jit(solution)/shard_map/all_to_all | solution.py:82
  291.8 18.9 %collective-permute-start.19 = (f32[192,384]{1,0:T(8,128)S(1)}, f32[192,384]{1,0:T(8,128)S(1)}, u32[]{:S(2)}, u32[]{:S(2)}) collective-permute-start(f32[192,384]{1,0:T(8,128)S(1)} %slice.205), channel_id=1, source_target_pairs={{0,32},{32,64},{64,96},{96,0},{1,33},{33,65},{65,97},{97,1},{2,34}... | collective-permute-start | bytes 884744 | tf_op jit(solution)/shard_map/ppermute | solution.py:15
  292.0 18.7 %collective-permute-start.20 = (f32[192,384]{1,0:T(8,128)S(1)}, f32[192,384]{1,0:T(8,128)S(1)}, u32[]{:S(2)}, u32[]{:S(2)}) collective-permute-start(f32[192,384]{1,0:T(8,128)S(1)} %slice.206), channel_id=1, source_target_pairs={{0,96},{32,0},{64,32},{96,64},{1,97},{33,1},{65,33},{97,65},{2,98}... | collective-permute-start | bytes 884744 | tf_op jit(solution)/shard_map/ppermute | solution.py:15
  295.8 20.0 %collective-permute-start.22 = (f32[384,384]{1,0:T(8,128)S(1)}, f32[384,384]{1,0:T(8,128)}, u32[]{:S(2)}, u32[]{:S(2)}) collective-permute-start(f32[384,384]{1,0:T(8,128)S(1)} %collective-permute-done.17), channel_id=1, source_target_pairs={{0,16},{16,0},{1,17},{17,1},{2,18},{18,2},{3,19},{19,3},{4,20},{20... | collective-permute-start | bytes 1769480 | tf_op jit(solution)/shard_map/ppermute | solution.py:15
  297.9 19.7 %collective-permute-start.23 = (f32[384,384]{1,0:T(8,128)S(1)}, f32[384,384]{1,0:T(8,128)}, u32[]{:S(2)}, u32[]{:S(2)}) collective-permute-start(f32[384,384]{1,0:T(8,128)S(1)} %collective-permute-done.18), channel_id=1, source_target_pairs={{0,16},{16,0},{1,17},{17,1},{2,18},{18,2},{3,19},{19,3},{4,20},{20... | collective-permute-start | bytes 1769480 | tf_op jit(solution)/shard_map/ppermute | solution.py:15
  (14 other events, 112.3 us)
Sparse Core Ops, SparseCore 0:
  60.3 77.9 all-gather.6
  141.0 100.0 all-gather.4
  243.3 75.4 all-gather.8
where the time goes:
time: 345 us; the launch traced here: 343 us
  waiting for transfers between devices  102 us (30%)
  between operations  89 us (26%)
  starting transfers between devices  62.1 us (18%)
  local copies, waits for them, and re-layouts  56.3 us (16%)
  matrix products  30.6 us (9%)
    ppermute x24, waiting for transfers between devices, shift(): return lax.ppermute(x, axis, [(i, (i + k) % n) for i in range(n)])  61.1 us
    ppermute x24, starting transfers between devices, shift(): return lax.ppermute(x, axis, [(i, (i + k) % n) for i in range(n)])  43.1 us
    dot_general x4, matrix products, dot(): lax.dot_general(a, b, (dims, ((), ())), precision=lax.Precision.HIGH, pre...  30.6 us
    dynamic_update_slice x8, local copies, waits for them, and re-layouts, per_device(): strip = lax.dynamic_update_slice(strip, t, (r * h, 0))  15.4 us
    all_to_all x2, waiting for transfers between devices, spread(): lax.all_to_all(x.reshape(3, 8, sub, w), ROW, 1, 0, tiled=True)  15.4 us
    unnamed x72, local copies, waits for them, and re-layouts  14.6 us
    ppermute x1, waiting for transfers between devices, per_device(): lax.ppermute(u, ALL, [(16 * r + c, 16 * (c // 2) + 2 * r + c % 2) for r i...  14.5 us
    all_gather x1, waiting for transfers between devices, per_device(): f_all = lax.all_gather(f, COL, axis=1, tiled=True)  11.1 us
  transfers between devices with their start and end apart: 31, of which 10 were waited for; matrix products, arithmetic and copies ran while one was open for 20% of the time, Pallas kernels for 0%

commit v1 on v0

--- a/solution.py
+++ b/solution.py
@@ -49,12 +49,13 @@
     sub = h // 24
     part = NANC * sub
     f = pick(spread(factor_cross), ancestors).reshape(part, w)
-    f_all = lax.all_gather(f, COL, axis=1, tiled=True)
     strip = jnp.zeros((8 * h, w), jnp.float32)
     for r, t in gather_rows(factor_inverse):
         strip = lax.dynamic_update_slice(strip, t, (r * h, 0))
     s = pick(spread(sigma_top), ancestors).reshape(part, w)
-    s_all = lax.all_gather(s, COL, axis=1, tiled=True)
+    f_all, s_all = jnp.split(
+        lax.all_gather(jnp.concatenate([f, s], 0), COL, axis=1, tiled=True), [f.shape[0]], 0
+    )
     u = dot(f_all, strip, ((1,), (0,)))
     moved = lax.ppermute(
         u, ALL, [(16 * r + c, 16 * (c // 2) + 2 * r + c % 2) for r in range(8) for c in range(16)]

time: 345 us -> 385 us (1.12)
  waiting for transfers between devices: 102 us -> 139 us
  starting transfers between devices: 62.1 us -> 73.6 us
  local copies, waits for them, and re-layouts: 56.3 us -> 46.9 us
    all_gather x2 -> x1, waiting for transfers between devices: 11.1 us -> 58.5 us  [per_device(): lax.all_gather(jnp.concatenate([f, s], 0), COL, axis=1, tiled=True)]
    unnamed x72 -> x68, local copies, waits for them, and re-layouts: 14.6 us -> 1.92 us
    ppermute x24, starting transfers between devices: 43.1 us -> 54.6 us  [shift(): return lax.ppermute(x, axis, [(i, (i + k) % n) for i in range(n)])]
    ppermute x1, waiting for transfers between devices: 14.5 us -> 7.57 us  [per_device(): lax.ppermute(u, ALL, [(16 * r + c, 16 * (c // 2) + 2 * r + c % 2) for r i...]
    split x0 -> x1, local copies, waits for them, and re-layouts: none -> 4.45 us  [per_device(): jnp.split(lax.all_gather(jnp.concatenate([f, s], 0), COL, axis=1, tiled=T...]
  transfers between devices with their start and end apart: 31 -> 30, of which waited for: 10 -> 9; matrix products, arithmetic and copies ran while one was open for 20% -> 13% of each run, Pallas kernels for 0% -> 0%
where the time goes in v1:
time: 385 us; the launch traced here: 383 us
  waiting for transfers between devices  139 us (36%)
  between operations  88.9 us (23%)
  starting transfers between devices  73.6 us (19%)
  local copies, waits for them, and re-layouts  46.9 us (12%)
  matrix products  30.6 us (8%)
  other arithmetic  4.08 us (1%)
    all_gather x1, waiting for transfers between devices, per_device(): lax.all_gather(jnp.concatenate([f, s], 0), COL, axis=1, tiled=True)  58.5 us
    ppermute x24, waiting for transfers between devices, shift(): return lax.ppermute(x, axis, [(i, (i + k) % n) for i in range(n)])  57.6 us
    ppermute x24, starting transfers between devices, shift(): return lax.ppermute(x, axis, [(i, (i + k) % n) for i in range(n)])  54.6 us
    dot_general x4, matrix products, dot(): lax.dot_general(a, b, (dims, ((), ())), precision=lax.Precision.HIGH, pre...  30.6 us
    all_to_all x2, waiting for transfers between devices, spread(): lax.all_to_all(x.reshape(3, 8, sub, w), ROW, 1, 0, tiled=True)  15.4 us
    dynamic_update_slice x8, local copies, waits for them, and re-layouts, per_device(): strip = lax.dynamic_update_slice(strip, t, (r * h, 0))  15.4 us
    all_to_all x2, starting transfers between devices, spread(): lax.all_to_all(x.reshape(3, 8, sub, w), ROW, 1, 0, tiled=True)  10.3 us
    dynamic_update_slice x7, local copies, waits for them, and re-layouts, per_device(): sigma_col = lax.dynamic_update_slice(sigma_col, t[None], (r, 0, 0))  10.3 us
  transfers between devices with their start and end apart: 30, of which 9 were waited for; matrix products, arithmetic and copies ran while one was open for 13% of the time, Pallas kernels for 0%

profile of v1, /device:TPU:1, one launch (start us, length us, event | category | flops | bytes accessed | tf_op | source)
XLA Modules:
  0.0 383.1 jit_solution(962950729751355335)
XLA Ops:
  9.6 6.0 %all-to-all-start.1 = ((f32[3,8,32,384]{3,2,0,1:T(8,128)}), f32[3,8,32,384]{3,2,0,1:T(8,128)S(1)}, u32[]{:S(2)}, u32[]{:S(2)}) async-start(f32[3,8,32,384]{3,2,0,1:T(8,128)} %copy.63), calls=%async_computation.1 | async-start | bytes 2359296 | tf_op jit(solution)/shard_map/all_to_all | solution.py:34
  16.7 15.4 %all-to-all-done.1 = f32[3,8,32,384]{3,2,0,1:T(8,128)S(1)} async-done(((f32[3,8,32,384]{3,2,0,1:T(8,128)}), f32[3,8,32,384]{3,2,0,1:T(8,128)S(1)}, u32[]{:S(2)}, u32[]{:S(2)}) %all-to-all-start.1) | async-done | bytes 1179680 | tf_op jit(solution)/shard_map/all_to_all | solution.py:34
  32.1 4.3 %all-to-all-start = ((f32[3,8,32,384]{3,2,0,1:T(8,128)}), f32[3,8,32,384]{3,2,0,1:T(8,128)S(1)}, u32[]{:S(2)}, u32[]{:S(2)}) async-start(f32[3,8,32,384]{3,2,0,1:T(8,128)} %copy.62), calls=%async_computation | async-start | bytes 2359296 | tf_op jit(solution)/shard_map/all_to_all | solution.py:34
  63.3 26.2 %collective-permute-done = f32[768,384]{1,0:T(8,128)S(1)} collective-permute-done((f32[768,384]{1,0:T(8,128)}, f32[768,384]{1,0:T(8,128)S(1)}, u32[]{:S(2)}, u32[]{:S(2)}) %collective-permute-start) | collective-permute-done | bytes 1179680 | tf_op jit(solution)/shard_map/ppermute | solution.py:15
  94.3 10.5 %collective-permute-done.2 = f32[384,384]{1,0:T(8,128)S(1)} collective-permute-done((f32[384,384]{1,0:T(8,128)S(1)}, f32[384,384]{1,0:T(8,128)S(1)}, u32[]{:S(2)}, u32[]{:S(2)}) %collective-permute-start.2) | collective-permute-done | bytes 589856 | tf_op jit(solution)/shard_map/ppermute | solution.py:15
  106.8 4.3 %broadcast_in_dim.53 = f32[6144,384]{1,0:T(8,128)} broadcast(f32[]{:T(128)} %constant.74.clone.1), dimensions={} | broadcast | bytes 9437188 | tf_op jit(solution)/shard_map/broadcast_in_dim | solution.py:52
  126.4 58.5 %all-gather.4.cloned.1.call-done = f32[768,6144]{1,0:T(8,128)} async-done(((f32[768,384]{1,0:T(8,128)}), f32[768,6144]{1,0:T(8,128)}) %all-gather.4.cloned.1.call-update) | async-done | bytes 18874384 | tf_op jit(solution)/shard_map/all_gather | solution.py:57
  184.9 11.7 %fusion = f32[384,384]{1,0:T(8,128)S(1)} fusion(f32[6144,384]{1,0:T(8,128)} %constant_dynamic-update-slice_fusion.62, f32[768,6144]{1,0:T(8,128)} %all-gather.4.cloned.1.call-done), kind=kOutput, calls=%fused_computation | convolution fusion | flops 5435817984 | bytes 19464192 | tf_op jit(solution)/shard_map/dot_general | solution.py:42
  196.6 5.1 %collective-permute-start.16 = (f32[384,384]{1,0:T(8,128)S(1)}, f32[384,384]{1,0:T(8,128)S(1)}, u32[]{:S(2)}, u32[]{:S(2)}) collective-permute-start(f32[384,384]{1,0:T(8,128)S(1)} %fusion), channel_id=1, source_target_pairs={{0,0},{1,1},{2,16},{3,17},{4,32},{5,33},{6,48},{7,49},{8,64},{9,65... | collective-permute-start | bytes 1769480 | tf_op jit(solution)/shard_map/ppermute | solution.py:60
  201.7 7.6 %collective-permute-done.16 = f32[384,384]{1,0:T(8,128)S(1)} collective-permute-done((f32[384,384]{1,0:T(8,128)S(1)}, f32[384,384]{1,0:T(8,128)S(1)}, u32[]{:S(2)}, u32[]{:S(2)}) %collective-permute-start.16) | collective-permute-done | bytes 589856 | tf_op jit(solution)/shard_map/ppermute | solution.py:60
  264.6 7.6 %collective-permute-start.8 = (f32[384,384]{1,0:T(8,128)S(1)}, f32[384,384]{1,0:T(8,128)S(1)}, u32[]{:S(2)}, u32[]{:S(2)}) collective-permute-start(f32[384,384]{1,0:T(8,128)S(1)} %fusion), channel_id=1, source_target_pairs={{0,32},{32,64},{64,96},{96,0},{1,33},{33,65},{65,97},{97,1},{2,34}... | collective-permute-start | bytes 1769480 | tf_op jit(solution)/shard_map/ppermute | solution.py:15
  272.2 5.2 %collective-permute-start.9 = (f32[384,384]{1,0:T(8,128)S(1)}, f32[384,384]{1,0:T(8,128)S(1)}, u32[]{:S(2)}, u32[]{:S(2)}) collective-permute-start(f32[384,384]{1,0:T(8,128)S(1)} %fusion), channel_id=1, source_target_pairs={{0,96},{32,0},{64,32},{96,64},{1,97},{33,1},{65,33},{97,65},{2,98}... | collective-permute-start | bytes 1769480 | tf_op jit(solution)/shard_map/ppermute | solution.py:15
  277.4 12.1 %collective-permute-start.12 = (f32[384,384]{1,0:T(8,128)S(1)}, f32[384,384]{1,0:T(8,128)S(1)}, u32[]{:S(2)}, u32[]{:S(2)}) collective-permute-start(f32[384,384]{1,0:T(8,128)S(1)} %fusion), channel_id=1, source_target_pairs={{0,16},{16,0},{1,17},{17,1},{2,18},{18,2},{3,19},{19,3},{4,20},{20... | collective-permute-start | bytes 1769480 | tf_op jit(solution)/shard_map/ppermute | solution.py:15
  289.5 4.5 %split.8 = f32[384,6144]{1,0:T(8,128)S(1)} slice(f32[768,6144]{1,0:T(8,128)} %all-gather.4.cloned.1.call-done), slice={[384:768], [0:6144]} | slice | bytes 18874368 | tf_op jit(solution)/shard_map/split | solution.py:56
  298.1 2.8 collective-permute-start.13
  302.9 3.1 collective-permute-start.15
  310.2 5.0 %bitcast_dynamic-update-slice_fusion.7 = (f32[8,384,384]{2,1,0:T(8,128)}, f32[384,384]{1,0:T(8,128)S(1)}) fusion(f32[8,384,384]{2,1,0:T(8,128)} %broadcast_in_dim.55, s32[]{:T(128)S(6)} %select_n.283, f32[384,3072]{1,0:T(8,128)S(1)} %dynamic-slice_dynamic-update-slice_fusion, f32[3072,384]{1,0:T(8,128)S(1)} %bitcast.118), kind=kOutput, calls=%fused_computation.18 | convolution fusion | flops 2718056448 | bytes 10616836 | tf_op jit(solution)/shard_map/dot_general | solution.py:42
  320.5 3.5 all-to-all-start.2
  324.0 7.2 %collective-permute-done.17 = f32[384,384]{1,0:T(8,128)S(1)} collective-permute-done((f32[384,384]{1,0:T(8,128)S(1)}, f32[384,384]{1,0:T(8,128)S(1)}, u32[]{:S(2)}, u32[]{:S(2)}) %collective-permute-start.17) | collective-permute-done | bytes 589856 | tf_op jit(solution)/shard_map/ppermute | solution.py:15
  331.4 3.8 collective-permute-start.20
  335.2 2.7 collective-permute-start.22
  339.6 10.5 %collective-permute-done.19 = f32[192,384]{1,0:T(8,128)S(1)} collective-permute-done((f32[192,384]{1,0:T(8,128)S(1)}, f32[192,384]{1,0:T(8,128)S(1)}, u32[]{:S(2)}, u32[]{:S(2)}) %collective-permute-start.19) | collective-permute-done | bytes 294944 | tf_op jit(solution)/shard_map/ppermute | solution.py:15
  361.3 7.8 %fusion.4 = f32[384,384]{1,0:T(8,128)S(1)} fusion(f32[8,384,384]{2,1,0:T(8,128)} %bitcast_dynamic-update-slice_fusion, f32[8,2,384,384]{3,2,1,0:T(8,128)} %bitcast.119), kind=kOutput, calls=%fused_computation.6 | convolution fusion | flops 2717908992 | bytes 10027008 | tf_op jit(solution)/shard_map/dot_general | solution.py:42
  369.0 6.1 %fusion.5 = f32[384,384]{1,0:T(8,128)S(1)} fusion(f32[8,384,384]{2,1,0:T(8,128)} %bitcast_dynamic-update-slice_fusion, f32[8,2,384,384]{3,2,1,0:T(8,128)S(1)} %bitcast.120), kind=kOutput, calls=%fused_computation.7 | convolution fusion | flops 2717908992 | bytes 10027008 | tf_op jit(solution)/shard_map/dot_general | solution.py:42
  (162 shorter events, 62.7 us)
Async XLA Ops:
  9.6 22.5 %all-to-all-start.1 = ((f32[3,8,32,384]{3,2,0,1:T(8,128)}), f32[3,8,32,384]{3,2,0,1:T(8,128)S(1)}, u32[]{:S(2)}, u32[]{:S(2)}) async-start(f32[3,8,32,384]{3,2,0,1:T(8,128)} %copy.63), calls=%async_computation.1 | async-start | bytes 2359296 | tf_op jit(solution)/shard_map/all_to_all | solution.py:34
  32.1 26.7 %all-to-all-start = ((f32[3,8,32,384]{3,2,0,1:T(8,128)}), f32[3,8,32,384]{3,2,0,1:T(8,128)S(1)}, u32[]{:S(2)}, u32[]{:S(2)}) async-start(f32[3,8,32,384]{3,2,0,1:T(8,128)} %copy.62), calls=%async_computation | async-start | bytes 2359296 | tf_op jit(solution)/shard_map/all_to_all | solution.py:34
  36.5 148.4 %all-gather.4.cloned.1.call-start = ((), (), s32[]{:S(2)}) async-start(), calls=%async_computation.3 | async-start | bytes 20054016 | tf_op jit(solution)/shard_map/all_gather | solution.py:57
  60.4 300.8 %all-gather.6.cloned.1.call-start = ((), (), s32[]{:S(2)}) async-start(), calls=%async_computation.4 | async-start | bytes 10027008 | tf_op jit(solution)/shard_map/all_gather | solution.py:63
  60.5 29.0 %collective-permute-start = (f32[768,384]{1,0:T(8,128)}, f32[768,384]{1,0:T(8,128)S(1)}, u32[]{:S(2)}, u32[]{:S(2)}) collective-permute-start(f32[768,384]{1,0:T(8,128)} %param.7), channel_id=1, source_target_pairs={{0,32},{32,64},{64,96},{96,0},{1,33},{33,65},{65,97},{97,1},{2,34}... | collective-permute-start | bytes 3538952 | tf_op jit(solution)/shard_map/ppermute | solution.py:15
  62.0 27.7 %collective-permute-start.1 = (f32[768,384]{1,0:T(8,128)}, f32[768,384]{1,0:T(8,128)S(1)}, u32[]{:S(2)}, u32[]{:S(2)}) collective-permute-start(f32[768,384]{1,0:T(8,128)} %param.7), channel_id=1, source_target_pairs={{0,96},{32,0},{64,32},{96,64},{1,97},{33,1},{65,33},{97,65},{2,98}... | collective-permute-start | bytes 3538952 | tf_op jit(solution)/shard_map/ppermute | solution.py:15
  89.6 15.3 %collective-permute-start.2 = (f32[384,384]{1,0:T(8,128)S(1)}, f32[384,384]{1,0:T(8,128)S(1)}, u32[]{:S(2)}, u32[]{:S(2)}) collective-permute-start(f32[384,384]{1,0:T(8,128)S(1)} %slice.200), channel_id=1, source_target_pairs={{0,32},{32,64},{64,96},{96,0},{1,33},{33,65},{65,97},{97,1},{2,34}... | collective-permute-start | bytes 1769480 | tf_op jit(solution)/shard_map/ppermute | solution.py:15
  89.7 15.2 %collective-permute-start.3 = (f32[384,384]{1,0:T(8,128)S(1)}, f32[384,384]{1,0:T(8,128)S(1)}, u32[]{:S(2)}, u32[]{:S(2)}) collective-permute-start(f32[384,384]{1,0:T(8,128)S(1)} %slice.201), channel_id=1, source_target_pairs={{0,96},{32,0},{64,32},{96,64},{1,97},{33,1},{65,33},{97,65},{2,98}... | collective-permute-start | bytes 1769480 | tf_op jit(solution)/shard_map/ppermute | solution.py:15
  92.4 24.4 %collective-permute-start.4 = (f32[768,384]{1,0:T(8,128)}, f32[768,384]{1,0:T(8,128)}, u32[]{:S(2)}, u32[]{:S(2)}) collective-permute-start(f32[768,384]{1,0:T(8,128)} %param.7), channel_id=1, source_target_pairs={{0,16},{16,0},{1,17},{17,1},{2,18},{18,2},{3,19},{19,3},{4,20},{20... | collective-permute-start | bytes 3538952 | tf_op jit(solution)/shard_map/ppermute | solution.py:15
  93.8 25.4 %collective-permute-start.5 = (f32[768,384]{1,0:T(8,128)S(1)}, f32[768,384]{1,0:T(8,128)}, u32[]{:S(2)}, u32[]{:S(2)}) collective-permute-start(f32[768,384]{1,0:T(8,128)S(1)} %collective-permute-done), channel_id=1, source_target_pairs={{0,16},{16,0},{1,17},{17,1},{2,18},{18,2},{3,19},{19,3},{4,20},{20... | collective-permute-start | bytes 3538952 | tf_op jit(solution)/shard_map/ppermute | solution.py:15
  93.8 27.8 %collective-permute-start.6 = (f32[768,384]{1,0:T(8,128)S(1)}, f32[768,384]{1,0:T(8,128)}, u32[]{:S(2)}, u32[]{:S(2)}) collective-permute-start(f32[768,384]{1,0:T(8,128)S(1)} %collective-permute-done.1), channel_id=1, source_target_pairs={{0,16},{16,0},{1,17},{17,1},{2,18},{18,2},{3,19},{19,3},{4,20},{20... | collective-permute-start | bytes 3538952 | tf_op jit(solution)/shard_map/ppermute | solution.py:15
  104.9 19.1 %collective-permute-start.7 = (f32[768,384]{1,0:T(8,128)S(1)}, f32[768,384]{1,0:T(8,128)}, u32[]{:S(2)}, u32[]{:S(2)}) collective-permute-start(f32[768,384]{1,0:T(8,128)S(1)} %constant_dynamic-update-slice_fusion.24), channel_id=1, source_target_pairs={{0,16},{16,0},{1,17},{17,1},{2,18},{18,2},{3,19},{19,3},{4,20},{20... | collective-permute-start | bytes 3538952 | tf_op jit(solution)/shard_map/ppermute | solution.py:15
  196.6 12.7 %collective-permute-start.16 = (f32[384,384]{1,0:T(8,128)S(1)}, f32[384,384]{1,0:T(8,128)S(1)}, u32[]{:S(2)}, u32[]{:S(2)}) collective-permute-start(f32[384,384]{1,0:T(8,128)S(1)} %fusion), channel_id=1, source_target_pairs={{0,0},{1,1},{2,16},{3,17},{4,32},{5,33},{6,48},{7,49},{8,64},{9,65... | collective-permute-start | bytes 1769480 | tf_op jit(solution)/shard_map/ppermute | solution.py:60
  264.6 30.5 %collective-permute-start.8 = (f32[384,384]{1,0:T(8,128)S(1)}, f32[384,384]{1,0:T(8,128)S(1)}, u32[]{:S(2)}, u32[]{:S(2)}) collective-permute-start(f32[384,384]{1,0:T(8,128)S(1)} %fusion), channel_id=1, source_target_pairs={{0,32},{32,64},{64,96},{96,0},{1,33},{33,65},{65,97},{97,1},{2,34}... | collective-permute-start | bytes 1769480 | tf_op jit(solution)/shard_map/ppermute | solution.py:15
  272.2 23.1 %collective-permute-start.9 = (f32[384,384]{1,0:T(8,128)S(1)}, f32[384,384]{1,0:T(8,128)S(1)}, u32[]{:S(2)}, u32[]{:S(2)}) collective-permute-start(f32[384,384]{1,0:T(8,128)S(1)} %fusion), channel_id=1, source_target_pairs={{0,96},{32,0},{64,32},{96,64},{1,97},{33,1},{65,33},{97,65},{2,98}... | collective-permute-start | bytes 1769480 | tf_op jit(solution)/shard_map/ppermute | solution.py:15
  277.4 28.7 %collective-permute-start.12 = (f32[384,384]{1,0:T(8,128)S(1)}, f32[384,384]{1,0:T(8,128)S(1)}, u32[]{:S(2)}, u32[]{:S(2)}) collective-permute-start(f32[384,384]{1,0:T(8,128)S(1)} %fusion), channel_id=1, source_target_pairs={{0,16},{16,0},{1,17},{17,1},{2,18},{18,2},{3,19},{19,3},{4,20},{20... | collective-permute-start | bytes 1769480 | tf_op jit(solution)/shard_map/ppermute | solution.py:15
  315.2 16.0 %collective-permute-start.17 = (f32[384,384]{1,0:T(8,128)S(1)}, f32[384,384]{1,0:T(8,128)S(1)}, u32[]{:S(2)}, u32[]{:S(2)}) collective-permute-start(f32[384,384]{1,0:T(8,128)S(1)} %get-tuple-element.41), channel_id=1, source_target_pairs={{0,32},{32,64},{64,96},{96,0},{1,33},{33,65},{65,97},{97,1},{2,34}... | collective-permute-start | bytes 1769480 | tf_op jit(solution)/shard_map/ppermute | solution.py:15
  315.4 15.9 %collective-permute-start.18 = (f32[384,384]{1,0:T(8,128)S(1)}, f32[384,384]{1,0:T(8,128)S(1)}, u32[]{:S(2)}, u32[]{:S(2)}) collective-permute-start(f32[384,384]{1,0:T(8,128)S(1)} %get-tuple-element.41), channel_id=1, source_target_pairs={{0,96},{32,0},{64,32},{96,64},{1,97},{33,1},{65,33},{97,65},{2,98}... | collective-permute-start | bytes 1769480 | tf_op jit(solution)/shard_map/ppermute | solution.py:15
  318.0 34.5 %collective-permute-start.21 = (f32[384,384]{1,0:T(8,128)S(1)}, f32[384,384]{1,0:T(8,128)}, u32[]{:S(2)}, u32[]{:S(2)}) collective-permute-start(f32[384,384]{1,0:T(8,128)S(1)} %get-tuple-element.41), channel_id=1, source_target_pairs={{0,16},{16,0},{1,17},{17,1},{2,18},{18,2},{3,19},{19,3},{4,20},{20... | collective-permute-start | bytes 1769480 | tf_op jit(solution)/shard_map/ppermute | solution.py:15
  320.5 33.9 %all-to-all-start.2 = ((f32[8,3,32,384]{3,2,1,0:T(8,128)}), f32[8,3,32,384]{3,2,1,0:T(8,128)S(1)}, u32[]{:S(2)}, u32[]{:S(2)}) async-start(f32[8,3,32,384]{3,2,1,0:T(8,128)} %broadcast_select_fusion), calls=%async_computation.2 | async-start | bytes 2359296 | tf_op jit(solution)/shard_map/all_to_all | solution.py:83
  331.2 18.9 %collective-permute-start.19 = (f32[192,384]{1,0:T(8,128)S(1)}, f32[192,384]{1,0:T(8,128)S(1)}, u32[]{:S(2)}, u32[]{:S(2)}) collective-permute-start(f32[192,384]{1,0:T(8,128)S(1)} %slice.205), channel_id=1, source_target_pairs={{0,32},{32,64},{64,96},{96,0},{1,33},{33,65},{65,97},{97,1},{2,34}... | collective-permute-start | bytes 884744 | tf_op jit(solution)/shard_map/ppermute | solution.py:15
  331.4 18.8 %collective-permute-start.20 = (f32[192,384]{1,0:T(8,128)S(1)}, f32[192,384]{1,0:T(8,128)S(1)}, u32[]{:S(2)}, u32[]{:S(2)}) collective-permute-start(f32[192,384]{1,0:T(8,128)S(1)} %slice.206), channel_id=1, source_target_pairs={{0,96},{32,0},{64,32},{96,64},{1,97},{33,1},{65,33},{97,65},{2,98}... | collective-permute-start | bytes 884744 | tf_op jit(solution)/shard_map/ppermute | solution.py:15
  335.2 20.3 %collective-permute-start.22 = (f32[384,384]{1,0:T(8,128)S(1)}, f32[384,384]{1,0:T(8,128)}, u32[]{:S(2)}, u32[]{:S(2)}) collective-permute-start(f32[384,384]{1,0:T(8,128)S(1)} %collective-permute-done.17), channel_id=1, source_target_pairs={{0,16},{16,0},{1,17},{17,1},{2,18},{18,2},{3,19},{19,3},{4,20},{20... | collective-permute-start | bytes 1769480 | tf_op jit(solution)/shard_map/ppermute | solution.py:15
  337.9 19.5 %collective-permute-start.23 = (f32[384,384]{1,0:T(8,128)S(1)}, f32[384,384]{1,0:T(8,128)}, u32[]{:S(2)}, u32[]{:S(2)}) collective-permute-start(f32[384,384]{1,0:T(8,128)S(1)} %collective-permute-done.18), channel_id=1, source_target_pairs={{0,16},{16,0},{1,17},{17,1},{2,18},{18,2},{3,19},{19,3},{4,20},{20... | collective-permute-start | bytes 1769480 | tf_op jit(solution)/shard_map/ppermute | solution.py:15
  (11 other events, 95.0 us)
Sparse Core Ops, SparseCore 0:
  60.6 124.2 all-gather.3
  210.2 93.8 all-gather.5
